TPU v7x, 32 devices: a whole 2x2x4 slice. The times are simulated.
32 devices in a mesh: dp: 16 (over z, y, core), seq: 2 (over x).
Axes of the slice: x: 2, y: 2, z: 4, core: 2. Of those that a mesh axis runs over, the one named last changes fastest.
Arguments:
- queries: bfloat16 [4096, 4096], P(('dp', 'seq')), may hold values from -180 to 180, as said below
- keys: bfloat16 [4096, 512], P(('dp', 'seq')), may hold values from -6 to 6, as said below
- values: bfloat16 [4096, 512], P(('dp', 'seq')), may hold values from -6 to 6
- lengths: int32 [16, 16], P('dp'), may hold values from 1 to 128, 256 in all within a row
- out_grad: bfloat16 [4096, 4096], P(('dp', 'seq')), may hold values from -6 to 6
Outputs:
- attended: bfloat16 [4096, 4096], P(('dp', 'seq'))
- query_grad: bfloat16 [4096, 4096], P(('dp', 'seq'))
- key_grad: bfloat16 [4096, 512], P(('dp', 'seq'))
- value_grad: bfloat16 [4096, 512], P(('dp', 'seq'))
Inputs may be any that keep to these rules, and one draw needn't show every extreme that they name: `queries`: queries stay within this range. `keys`: keys stay within this range.
All inputs are finite; a program needn't handle non-finite values.
Results may differ from a plain program's by a relative error of at most 0.0095.
Values may be sent and summed in bfloat16 or wider, within the bound.
A program may use at most 64 MiB of HBM per device.

v0:
```python
import functools

import jax
import jax.numpy as jnp
from jax import lax
from jax.experimental import pallas as pl
from jax.experimental.pallas import tpu as pltpu
from jax.sharding import PartitionSpec as P

H = 32
KVH = 4
HD = 128
GROUP = 8
SCALE = HD ** (-0.5)
EXP2_SCALE = SCALE * 1.4426950408889634
NT = (((1,), (1,)), ((), ()))
NN = (((1,), (0,)), ((), ()))


def dot(a, b, dims):
    return lax.dot_general(a, b, dims, preferred_element_type=jnp.float32)


def lanes(index, width):
    return pl.ds(pl.multiple_of(index * width, 128), width)


def kernel(
    n, rows, segs,
    lens_in, q_in, k_in, v_in, g_in,
    att_out, dq_out, dk_out, dv_out,
    lens, q, g, qt, gt, att, dq, bias,
    kv, part, got, own,
    lens_sem, load_sem, own_sem, store_sem, final_sem,
    kv_send, kv_recv, part_send, part_recv,
):
    me = lax.axis_index("seq")
    lens_copy = pltpu.make_async_copy(lens_in, lens, lens_sem)
    lens_copy.start()
    barrier = pltpu.get_barrier_semaphore()
    for step in range(1, n):
        pl.semaphore_signal(
            barrier, inc=1, device_id={"seq": lax.rem(me + step, n)},
            device_id_type=pl.DeviceIdType.MESH,
        )

    wide = GROUP * HD
    sources = (k_in, v_in)

    def load(which, k):
        return pltpu.make_async_copy(
            (q_in, g_in)[which].at[:, lanes(k, wide)],
            (q, g)[which].at[:, lanes(k, wide)],
            load_sem.at[which, k],
        )

    def store(which, k):
        return pltpu.make_async_copy(
            (att, dq)[which].at[:, lanes(k, wide)],
            (att_out, dq_out)[which].at[:, lanes(k, wide)],
            store_sem.at[which, k],
        )

    def send_kv(which, k, src, dst):
        return pltpu.make_async_remote_copy(
            src_ref=sources[which].at[:, lanes(k, HD)],
            dst_ref=kv.at[which, pl.ds(src * rows, rows), lanes(k, HD)],
            send_sem=kv_send.at[which, k, dst],
            recv_sem=kv_recv.at[which, k, src],
            device_id={"seq": dst},
            device_id_type=pl.DeviceIdType.MESH,
        )

    def send_part(which, k, src, dst):
        return pltpu.make_async_remote_copy(
            src_ref=part.at[which, pl.ds(dst * rows, rows), lanes(k, HD)],
            dst_ref=got.at[which, pl.ds(src * rows, rows), lanes(k, HD)],
            send_sem=part_send.at[which, k, dst],
            recv_sem=part_recv.at[which, k, src],
            device_id={"seq": dst},
            device_id_type=pl.DeviceIdType.MESH,
        )

    def on_device(m):
        length = (m + 1) * rows
        heads = GROUP
        while heads > 1 and heads * rows * length > 1 << 18:
            heads //= 2

        own_copies = [
            pltpu.make_async_copy(
                sources[which], kv.at[which, pl.ds(m * rows, rows), :], own_sem.at[which]
            )
            for which in range(2)
        ]
        for which in range(2):
            own_copies[which].start()
        for k in range(KVH):
            load(0, k).start()
            load(1, k).start()
        pl.semaphore_wait(barrier, n - 1)
        for k in range(KVH):
            for dst in range(m + 1, n):
                send_kv(0, k, m, dst).start()
                send_kv(1, k, m, dst).start()

        lens_copy.wait()
        pos = lax.broadcasted_iota(jnp.int32, (rows, 128), 0) + m * rows
        first = jnp.zeros((rows, 128), jnp.int32)
        end = jnp.int32(0)
        for seg in range(segs):
            end = end + lens[0, seg]
            first = jnp.maximum(first, jnp.where(pos >= end, end, 0))
        for c in range(length // 128):
            col = lax.broadcasted_iota(jnp.int32, (rows, 128), 1) + c * 128
            seen = (col >= first) & (col <= pos)
            bias[:, c * 128:(c + 1) * 128] = jnp.where(seen, 0.0, -1e30)

        @pl.loop(0, KVH)
        def _(k):
            load(0, k).wait()
            load(1, k).wait()
            for h in range(GROUP):
                head = k * GROUP + h
                qt[:, lanes(head, rows)] = q[:, lanes(head, HD)].T
                gt[:, lanes(head, rows)] = g[:, lanes(head, HD)].T

        for which in range(2):
            own_copies[which].wait()

        @pl.loop(0, KVH)
        def _(k):
            for src in range(m):
                send_kv(0, k, src, src).wait_recv()
                send_kv(1, k, src, src).wait_recv()
            key = kv[0, 0:length, lanes(k, HD)]
            value = kv[1, 0:length, lanes(k, HD)]
            dkt = jnp.zeros((HD, length), jnp.float32)
            dvt = jnp.zeros((HD, length), jnp.float32)
            for base in range(0, GROUP, heads):
                ids = [k * GROUP + base + h for h in range(heads)]
                qs = jnp.concatenate([q[:, lanes(i, HD)] for i in ids], axis=0)
                gs = jnp.concatenate([g[:, lanes(i, HD)] for i in ids], axis=0)
                raw = dot(qs, key, NT).reshape(heads, rows, length)
                raw = (raw + bias[:, 0:length][None]).reshape(heads * rows, length)
                top = jnp.max(raw, axis=-1, keepdims=True)
                expo = jnp.exp2((raw - top) * EXP2_SCALE)
                inv = 1.0 / jnp.sum(expo, axis=-1, keepdims=True)
                out = (dot(expo.astype(jnp.bfloat16), value, NN) * inv).astype(jnp.bfloat16)
                rowdot = jnp.sum(
                    gs.astype(jnp.float32) * out.astype(jnp.float32), axis=-1, keepdims=True
                )
                probs = expo * inv
                dscores = (probs * (dot(gs, value, NT) - rowdot)).astype(jnp.bfloat16)
                grad = (dot(dscores, key, NN) * SCALE).astype(jnp.bfloat16)
                for h in range(heads):
                    att[:, lanes(ids[h], HD)] = out[h * rows:(h + 1) * rows]
                    dq[:, lanes(ids[h], HD)] = grad[h * rows:(h + 1) * rows]
                span = pl.ds(pl.multiple_of(ids[0] * rows, 128), heads * rows)
                dkt += dot(qt[:, span], dscores, NN)
                dvt += dot(gt[:, span], probs.astype(jnp.bfloat16), NN)
            part[0, 0:length, lanes(k, HD)] = (dkt.T * SCALE).astype(jnp.bfloat16)
            part[1, 0:length, lanes(k, HD)] = dvt.T.astype(jnp.bfloat16)
            for dst in range(m):
                send_part(0, k, m, dst).start()
                send_part(1, k, m, dst).start()
            store(0, k).start()
            store(1, k).start()

        mine = pl.ds(m * rows, rows)
        finals = []
        for which in range(2):
            final = part.at[which, mine, :]
            if m < n - 1:
                final = own.at[which]
            finals.append(
                pltpu.make_async_copy(final, (dk_out, dv_out)[which], final_sem.at[which])
            )
        if m < n - 1:
            for k in range(KVH):
                for which in range(2):
                    total = part[which, mine, lanes(k, HD)].astype(jnp.float32)
                    for src in range(m + 1, n):
                        send_part(which, k, src, src).wait_recv()
                        total += got[which, pl.ds(src * rows, rows), lanes(k, HD)].astype(
                            jnp.float32
                        )
                    own[which, :, lanes(k, HD)] = total.astype(jnp.bfloat16)
        for which in range(2):
            finals[which].start()
        for k in range(KVH):
            for which in range(2):
                store(which, k).wait()
                for dst in range(m + 1, n):
                    send_kv(which, k, m, dst).wait_send()
                for dst in range(m):
                    send_part(which, k, m, dst).wait_send()
        for which in range(2):
            finals[which].wait()

    for m in range(n):
        pl.when(me == m)(functools.partial(on_device, m))


def write_out(*refs):
    sources, targets, sem = refs[:4], refs[4:8], refs[8]
    copies = []
    for index in range(4):
        pieces = 4 if index < 2 else 1
        step = sources[index].shape[0] // pieces
        for piece in range(pieces):
            part = pl.ds(piece * step, step)
            copies.append(
                pltpu.make_async_copy(
                    sources[index].at[part], targets[index].at[part], sem.at[index, piece]
                )
            )
    for copy in copies:
        copy.start()
    for copy in copies:
        copy.wait()


def shards(n, queries, keys, values, lengths, out_grad):
    rows = queries.shape[0]
    segs = lengths.shape[1]
    total = n * rows
    bf16 = jnp.bfloat16
    dma = pltpu.SemaphoreType.DMA
    wide = jax.ShapeDtypeStruct(queries.shape, bf16)
    thin = jax.ShapeDtypeStruct(keys.shape, bf16)
    anywhere = pl.BlockSpec(memory_space=pl.ANY)
    held = pl.pallas_call(
        functools.partial(kernel, n, rows, segs),
        out_shape=(wide, wide, thin, thin),
        in_specs=[pl.BlockSpec(memory_space=pltpu.HBM)] * 5,
        out_specs=(anywhere,) * 4,
        scratch_shapes=[
            pltpu.SMEM(lengths.shape, jnp.int32),
            pltpu.VMEM((rows, H * HD), bf16),
            pltpu.VMEM((rows, H * HD), bf16),
            pltpu.VMEM((HD, H * rows), bf16),
            pltpu.VMEM((HD, H * rows), bf16),
            pltpu.VMEM((rows, H * HD), bf16),
            pltpu.VMEM((rows, H * HD), bf16),
            pltpu.VMEM((rows, total), jnp.float32),
            pltpu.VMEM((2, total, KVH * HD), bf16),
            pltpu.VMEM((2, total, KVH * HD), bf16),
            pltpu.VMEM((2, total, KVH * HD), bf16),
            pltpu.VMEM((2, rows, KVH * HD), bf16),
            dma(()),
            dma((2, KVH)),
            dma((2,)),
            dma((2, KVH)),
            dma((2,)),
            dma((2, KVH, n)),
            dma((2, KVH, n)),
            dma((2, KVH, n)),
            dma((2, KVH, n)),
        ],
        compiler_params=pltpu.CompilerParams(
            collective_id=0, has_side_effects=True, vmem_limit_bytes=48 * 1024 * 1024
        ),
    )(*(
        pltpu.with_memory_space_constraint(x, pltpu.HBM)
        for x in (lengths, queries, keys, values, out_grad)
    ))
    return pl.pallas_call(
        write_out,
        out_shape=(wide, wide, thin, thin),
        in_specs=[anywhere] * 4,
        out_specs=(pl.BlockSpec(memory_space=pltpu.HBM),) * 4,
        scratch_shapes=[dma((4, 4))],
        compiler_params=pltpu.CompilerParams(vmem_limit_bytes=1024 * 1024),
    )(*(pltpu.with_memory_space_constraint(x, pltpu.VMEM) for x in held))


def solution(mesh):
    rows = P(("dp", "seq"), None)
    return jax.shard_map(
        functools.partial(shards, mesh.shape["seq"]),
        mesh=mesh,
        in_specs=(rows, rows, rows, P("dp", None), rows),
        out_specs=(rows,) * 4,
        check_vma=False,
    )
```

profile of v0, /device:TPU:0, one launch (start us, length us, event | category | flops | bytes accessed | tf_op | source)
XLA Modules:
  0.0 19.4 jit_solution(10536034359658978616)
XLA Ops:
  0.6 17.2 %shard_map.84 = (bf16[128,4096]{1,0:T(8,128)(2,1)S(1)}, bf16[128,4096]{1,0:T(8,128)(2,1)S(1)}, bf16[128,512]{1,0:T(8,128)(2,1)S(1)}, bf16[128,512]{1,0:T(8,128)(2,1)S(1)}) custom-call(s32[1,16]{1,0:T(1,128)} %lens_in.1, bf16[128,4096]{1,0:T(8,128)(2,1)} %q_in.1, bf16[128,512]{1,0:T(8,128)(2,1)} %k_in.1, bf16[128,512]{1,0:T(8,128)(2,1)} %v_in.1, ...), custom_call_target="tpu_custom_call" | custom-call | tf_op jit(solution)/shard_map/pallas_call | solution.py:233
  17.8 1.5 %shard_map.85 = (bf16[128,4096]{1,0:T(8,128)(2,1)}, bf16[128,4096]{1,0:T(8,128)(2,1)}, bf16[128,512]{1,0:T(8,128)(2,1)}, bf16[128,512]{1,0:T(8,128)(2,1)}) custom-call(bf16[128,4096]{1,0:T(8,128)(2,1)S(1)} %get-tuple-element.8.refs_0_, bf16[128,4096]{1,0:T(8,128)(2,1)S(1)} %get-tuple-element.9.refs_1_, bf16[128,512]{1,0:T(8,128)(2,1)S(1)} %get-tuple-element.10.refs_2_, ...), custom_call_target="tpu_custom_call" | custom-call | tf_op jit(solution)/shard_map/pallas_call | solution.py:268
where the time goes:
time: 19.5 us; the launch traced here: 19.4 us
  Pallas kernels  18.7 us (96%)
  between operations  0.64 us (3%)
    pallas_call x1, Pallas kernels, shards(): pl.pallas_call(functools.partial(kernel, n, rows, segs), out_shape=(wide,...  17.2 us
    pallas_call x1, Pallas kernels, shards(): pl.pallas_call(write_out, out_shape=(wide, wide, thin, thin), in_specs=[a...  1.53 us

commit v1 on v0

--- a/solution.py
+++ b/solution.py
@@ -28,10 +28,10 @@
 def kernel(
     n, rows, segs,
     lens_in, q_in, k_in, v_in, g_in,
-    att_out, dq_out, dk_out, dv_out,
-    lens, q, g, qt, gt, att, dq, bias,
-    kv, part, got, own,
-    lens_sem, load_sem, own_sem, store_sem, final_sem,
+    att, dq, dk, dv,
+    lens, q, g, qt, gt, bias,
+    kv, part, got,
+    lens_sem, load_sem, own_sem,
     kv_send, kv_recv, part_send, part_recv,
 ):
     me = lax.axis_index("seq")
@@ -54,13 +54,6 @@
             load_sem.at[which, k],
         )
 
-    def store(which, k):
-        return pltpu.make_async_copy(
-            (att, dq)[which].at[:, lanes(k, wide)],
-            (att_out, dq_out)[which].at[:, lanes(k, wide)],
-            store_sem.at[which, k],
-        )
-
     def send_kv(which, k, src, dst):
         return pltpu.make_async_remote_copy(
             src_ref=sources[which].at[:, lanes(k, HD)],
@@ -84,7 +77,7 @@
     def on_device(m):
         length = (m + 1) * rows
         heads = GROUP
-        while heads > 1 and heads * rows * length > 1 << 18:
+        while heads > 1 and heads * rows * length > 1 << 16:
             heads //= 2
 
         own_copies = [
@@ -164,18 +157,8 @@
             for dst in range(m):
                 send_part(0, k, m, dst).start()
                 send_part(1, k, m, dst).start()
-            store(0, k).start()
-            store(1, k).start()
 
         mine = pl.ds(m * rows, rows)
-        finals = []
-        for which in range(2):
-            final = part.at[which, mine, :]
-            if m < n - 1:
-                final = own.at[which]
-            finals.append(
-                pltpu.make_async_copy(final, (dk_out, dv_out)[which], final_sem.at[which])
-            )
         if m < n - 1:
             for k in range(KVH):
                 for which in range(2):
@@ -185,18 +168,16 @@
                         total += got[which, pl.ds(src * rows, rows), lanes(k, HD)].astype(
                             jnp.float32
                         )
-                    own[which, :, lanes(k, HD)] = total.astype(jnp.bfloat16)
-        for which in range(2):
-            finals[which].start()
+                    (dk, dv)[which][:, lanes(k, HD)] = total.astype(jnp.bfloat16)
+        else:
+            dk[...] = part[0, mine, :]
+            dv[...] = part[1, mine, :]
         for k in range(KVH):
             for which in range(2):
-                store(which, k).wait()
                 for dst in range(m + 1, n):
                     send_kv(which, k, m, dst).wait_send()
                 for dst in range(m):
                     send_part(which, k, m, dst).wait_send()
-        for which in range(2):
-            finals[which].wait()
 
     for m in range(n):
         pl.when(me == m)(functools.partial(on_device, m))
@@ -232,25 +213,20 @@
     anywhere = pl.BlockSpec(memory_space=pl.ANY)
     held = pl.pallas_call(
         functools.partial(kernel, n, rows, segs),
-        out_shape=(wide, wide, thin, thin),
+        out_shape=tuple(pltpu.VMEM(x.shape, bf16) for x in (wide, wide, thin, thin)),
         in_specs=[pl.BlockSpec(memory_space=pltpu.HBM)] * 5,
-        out_specs=(anywhere,) * 4,
+        out_specs=(pl.BlockSpec(memory_space=pltpu.VMEM),) * 4,
         scratch_shapes=[
             pltpu.SMEM(lengths.shape, jnp.int32),
             pltpu.VMEM((rows, H * HD), bf16),
             pltpu.VMEM((rows, H * HD), bf16),
             pltpu.VMEM((HD, H * rows), bf16),
             pltpu.VMEM((HD, H * rows), bf16),
-            pltpu.VMEM((rows, H * HD), bf16),
-            pltpu.VMEM((rows, H * HD), bf16),
             pltpu.VMEM((rows, total), jnp.float32),
             pltpu.VMEM((2, total, KVH * HD), bf16),
             pltpu.VMEM((2, total, KVH * HD), bf16),
             pltpu.VMEM((2, total, KVH * HD), bf16),
-            pltpu.VMEM((2, rows, KVH * HD), bf16),
             dma(()),
-            dma((2, KVH)),
-            dma((2,)),
             dma((2, KVH)),
             dma((2,)),
             dma((2, KVH, n)),

time: 19.5 us -> 22.4 us (1.15)
  Pallas kernels: 18.7 us -> 21.6 us
    pallas_call x1, Pallas kernels: 17.2 us -> 20.1 us  [shards(): pl.pallas_call(functools.partial(kernel, n, rows, segs), out_shape=tuple(...]
where the time goes in v1:
time: 22.4 us; the launch traced here: 22.2 us
  Pallas kernels  21.6 us (96%)
  between operations  0.64 us (3%)
    pallas_call x1, Pallas kernels, shards(): pl.pallas_call(functools.partial(kernel, n, rows, segs), out_shape=tuple(...  20.1 us
    pallas_call x1, Pallas kernels, shards(): pl.pallas_call(write_out, out_shape=(wide, wide, thin, thin), in_specs=[a...  1.53 us

profile of v1, /device:TPU:0, one launch (start us, length us, event | category | flops | bytes accessed | tf_op | source)
XLA Modules:
  0.0 22.2 jit_solution(5913602297546469188)
XLA Ops:
  0.6 20.1 %shard_map.84 = (bf16[128,4096]{1,0:T(8,128)(2,1)S(1)}, bf16[128,4096]{1,0:T(8,128)(2,1)S(1)}, bf16[128,512]{1,0:T(8,128)(2,1)S(1)}, bf16[128,512]{1,0:T(8,128)(2,1)S(1)}) custom-call(s32[1,16]{1,0:T(1,128)} %lens_in.1, bf16[128,4096]{1,0:T(8,128)(2,1)} %q_in.1, bf16[128,512]{1,0:T(8,128)(2,1)} %k_in.1, bf16[128,512]{1,0:T(8,128)(2,1)} %v_in.1, ...), custom_call_target="tpu_custom_call" | custom-call | tf_op jit(solution)/shard_map/pallas_call | solution.py:214
  20.7 1.5 %shard_map.85 = (bf16[128,4096]{1,0:T(8,128)(2,1)}, bf16[128,4096]{1,0:T(8,128)(2,1)}, bf16[128,512]{1,0:T(8,128)(2,1)}, bf16[128,512]{1,0:T(8,128)(2,1)}) custom-call(bf16[128,4096]{1,0:T(8,128)(2,1)S(1)} %get-tuple-element.8.refs_0_, bf16[128,4096]{1,0:T(8,128)(2,1)S(1)} %get-tuple-element.9.refs_1_, bf16[128,512]{1,0:T(8,128)(2,1)S(1)} %get-tuple-element.10.refs_2_, ...), custom_call_target="tpu_custom_call" | custom-call | tf_op jit(solution)/shard_map/pallas_call | solution.py:244
